TPU v7x, 512 devices: a whole 4x4x16 slice. The times are simulated.
512 devices in a mesh: cd: 64 (over z, y_lo, core), ab: 8 (over y_hi, x).
Axes of the slice: x: 4, y: 4 (y_hi: 2, y_lo: 2; y = y_hi * 2 + y_lo), z: 16, core: 2. Of those that a mesh axis runs over, the one named last changes fastest.
Arguments:
- amplitudes: float32 [2048, 32768], P(('cd', 'ab')), may hold values from -6 to 6
- integrals: float32 [4096, 32768], P('ab', 'cd'), may hold values from -0.09375 to 0.09375
- orbital_irrep: int32 [1600], replicated, may hold values from 0 to 7
- bra_pairs: int32 [2, 4096], P(None, 'ab'), may hold values from 0 to 1599
- ket_pairs: int32 [2, 32768], P(None, 'cd'), may hold values from 0 to 1599
- slot_pair: int32 [2048], replicated, may hold values from 0 to 2047, each once
Outputs:
- residual: float32 [2048, 4096], P('cd', 'ab')
Inputs may be any that keep to these rules, and one draw needn't show every extreme that they name: `slot_pair`: each value appears once; values of 1830 and above mark empty slots.
All inputs are finite; a program needn't handle non-finite values.
Results may differ from a plain program's by a relative error of at most 0.0003.
Values sent between devices are 32-bit elements; how exact they have to be, the bound alone decides.
A program may use at most 64 MiB of HBM per device.

v0:
```python
import jax
import jax.numpy as jnp
from jax import lax
from jax.sharding import PartitionSpec as P

PAIRS = 1830


def on_device(amplitudes, integrals, orbital_irrep, bra_pairs, ket_pairs, slot_pair):
    cd_count = lax.axis_size("cd")
    ab_count = lax.axis_size("ab")
    slot_block = amplitudes.shape[0]
    slot_total = slot_block * cd_count * ab_count
    bra_irrep = jnp.bitwise_xor(orbital_irrep[bra_pairs[0]], orbital_irrep[bra_pairs[1]])
    ket_irrep = jnp.bitwise_xor(orbital_irrep[ket_pairs[0]], orbital_irrep[ket_pairs[1]])
    selected = jnp.where(
        bra_irrep[:, None] == ket_irrep[None, :], integrals, jnp.zeros_like(integrals)
    )
    slot_ids = jnp.arange(slot_total, dtype=jnp.int32)
    cd_slabs = lax.all_to_all(amplitudes, "cd", split_axis=1, concat_axis=0, tiled=True)
    partial_value = lax.dot_general(
        lax.all_gather(cd_slabs, "ab", axis=0, tiled=True),
        selected,
        (((1,), (1,)), ((), ())),
        precision=lax.Precision.HIGHEST,
        preferred_element_type=jnp.float32,
    )
    group_rows = slot_block * ab_count
    position = (
        slot_ids // slot_block % ab_count * (slot_block * cd_count)
        + slot_ids // group_rows * slot_block
        + slot_ids % slot_block
    )
    inverse = jnp.zeros((slot_total,), jnp.int32).at[slot_pair].set(slot_ids)
    ordered = partial_value[position[inverse]]
    keep = slot_ids[:, None] < PAIRS
    ordered = jnp.where(keep, ordered, jnp.zeros_like(ordered))
    return lax.psum_scatter(ordered, "cd", scatter_dimension=0, tiled=True)


def solution(mesh):
    in_specs = (P(("cd", "ab"), None), P("ab", "cd"), P(), P(None, "ab"), P(None, "cd"), P())
    out_specs = P("cd", "ab")
    return jax.shard_map(
        on_device, mesh=mesh, in_specs=in_specs, out_specs=out_specs, check_vma=False
    )
```

profile of v0, /device:TPU:2, one launch (start us, length us, event | category | flops | bytes accessed | tf_op | source)
XLA Modules:
  0.0 406.0 jit_solution(12027138343469716382)
XLA Ops:
  6.5 0.0 copy-start
  6.5 0.0 copy-start.3
  6.5 0.0 all-gather.2.cloned.1.call-start
  6.5 50.9 %all_to_all.19 = f32[4,64,512]{2,0,1:T(4,128)S(1)} all-to-all(f32[4,64,512]{2,0,1:T(4,128)} %bitcast.20), channel_id=1, replica_groups=mesh['cd'=64,'ab'=8] {'cd'}, dimensions={1} | all-to-all | bytes 1048576 | tf_op jit(solution)/shard_map/all_to_all | solution.py:20
  57.5 1.0 all_to_all.17
  58.5 0.0 all-gather.2.cloned.1.call-update
  58.5 0.0 reduce-scatter.2.cloned.1.call-start
  58.5 0.8 compare_select_fusion.5
  59.3 0.0 copy-done
  59.3 0.0 copy-start.2
  59.4 3.1 gather_fusion
  62.5 3.1 gather_fusion.1
  65.7 0.0 copy-done.3
  65.7 3.1 gather_fusion.2
  68.9 3.1 gather_fusion.3
  72.0 0.0 copy-done.2
  72.1 8.0 %scatter_custom_fusion = s32[2048]{0:T(1024)S(1)} fusion(s32[2048]{0:T(1024)S(1)} %compare_select_fusion.2, s32[2048]{0:T(1024)S(1)} %iota.11, s32[]{:T(128)} %constant.55.clone.1), kind=kCustom, calls=%fused_computation.52 | custom fusion | bytes 8196 | tf_op jit(solution)/shard_map/scatter | solution.py:34
  80.2 0.0 copy-start.1
  80.2 11.8 %gather_fusion.4 = s32[2048]{0:T(1024)S(1)} fusion(s32[2048]{0:T(1024)S(1)} %get-tuple-element.9, s32[2048]{0:T(1024)S(1)} %get-tuple-element.10), kind=kCustom, calls=%fused_computation.4 | custom fusion | bytes 24576 | tf_op jit(solution)/shard_map/gather | solution.py:35
  92.0 44.0 %all-gather.2.cloned.1.call-done = f32[2048,512]{1,0:T(8,128)} async-done(((f32[256,512]{1,0:T(8,128)}), f32[2048,512]{1,0:T(8,128)}) %all-gather.2.cloned.1.call-update) | async-done | bytes 4194320 | tf_op jit(solution)/shard_map/all_gather | solution.py:22
  136.0 0.0 copy-done.1
  136.0 10.2 %convolution_bitcast_fusion = f32[2048,512]{0,1:T(8,128)} fusion(f32[2048,512]{1,0:T(8,128)} %all-gather.2.cloned.1.call-done, f32[512,512]{1,0:T(8,128)S(1)} %copy-done.1, s32[512]{0:T(512)S(1)} %xor.15, s32[512]{0:T(512)S(1)} %xor.14), kind=kOutput, calls=%fused_computation.7 | convolution fusion | flops 6442975232 | bytes 9441280 | tf_op jit(solution)/shard_map/dot_general | solution.py:21
  146.2 5.3 %copy.9 = f32[2048,512]{1,0:T(8,128)} copy(f32[2048,512]{0,1:T(8,128)} %convolution_bitcast_fusion) | data formatting | bytes 8388608 | tf_op jit(solution)/shard_map/dot_general | solution.py:21
  151.6 11.8 %gather_fusion.5 = f32[2048,512]{1,0:T(8,128)} fusion(f32[2048,512]{1,0:T(8,128)} %copy.9, s32[2048]{0:T(1024)S(1)} %broadcast_clamp_fusion), kind=kCustom, calls=%fused_computation.5 | custom fusion | bytes 8396800 | tf_op jit(solution)/shard_map/gather | solution.py:35
  163.3 3.8 broadcast_select_fusion
  167.1 0.0 reduce-scatter.2.cloned.1.call-update
  167.2 232.0 %reduce-scatter.2.cloned.1.call-done = f32[32,512]{1,0:T(8,128)} async-done(((f32[2048,512]{1,0:T(8,128)}), f32[32,512]{1,0:T(8,128)}) %reduce-scatter.2.cloned.1.call-update) | async-done | bytes 65552 | tf_op jit(solution)/shard_map/reduce_scatter | solution.py:38
  (13 shorter events, 0.1 us)
Async XLA Ops:
  6.5 52.8 %copy-start = (s32[1600]{0:T(1024)S(1)}, s32[1600]{0:T(1024)}, u32[]{:S(2)}) copy-start(s32[1600]{0:T(1024)} %param.8) | copy-start | bytes 19204
  6.5 59.1 %copy-start.3 = (s32[2,512]{1,0:T(2,128)S(1)}, s32[2,512]{1,0:T(2,128)}, u32[]{:S(2)}) copy-start(s32[2,512]{1,0:T(2,128)} %param.10) | copy-start | bytes 12292
  6.5 129.4 %all-gather.2.cloned.1.call-start = ((), (), s32[]{:S(2)}) async-start(), calls=%async_computation.2 | async-start | bytes 4718592 | tf_op jit(solution)/shard_map/all_gather | solution.py:22
  58.5 340.6 %reduce-scatter.2.cloned.1.call-start = ((), (), s32[]{:S(2)}) async-start(), calls=%async_computation.3 | async-start | bytes 4259840 | tf_op jit(solution)/shard_map/reduce_scatter | solution.py:38
  59.3 12.7 %copy-start.2 = (s32[2048]{0:T(1024)S(1)}, s32[2048]{0:T(1024)}, u32[]{:S(2)}) copy-start(s32[2048]{0:T(1024)} %param.11) | copy-start | bytes 24580
  80.2 55.8 %copy-start.1 = (f32[512,512]{1,0:T(8,128)S(1)}, f32[512,512]{1,0:T(8,128)}, u32[]{:S(2)}) copy-start(f32[512,512]{1,0:T(8,128)} %param.7) | copy-start | bytes 3145732
Sparse Core Ops, SparseCore 0:
  58.6 77.3 all-gather.1
  167.3 231.8 reduce-scatter.1
where the time goes:
time: 406 us
  waiting for transfers between devices  276 us (68%)
  blocking collectives  50.9 us (13%)
  local copies, waits for them, and re-layouts  50.5 us (12%)
  between operations  13.6 us (3%)
  matrix products  10.2 us (3%)
  other arithmetic  4.65 us (1%)
    reduce_scatter x1, waiting for transfers between devices, on_device(): return lax.psum_scatter(ordered, 'cd', scatter_dimension=0, tiled=True)  232 us
    all_to_all x1, blocking collectives, on_device(): lax.all_to_all(amplitudes, 'cd', split_axis=1, concat_axis=0, tiled=True)  50.9 us
    all_gather x1, waiting for transfers between devices, on_device(): lax.all_gather(cd_slabs, 'ab', axis=0, tiled=True)  44 us
    gather x2, local copies, waits for them, and re-layouts, on_device(): ordered = partial_value[position[inverse]]  23.5 us
    dot_general x1, matrix products, on_device(): lax.dot_general(lax.all_gather(cd_slabs, 'ab', axis=0, tiled=True), selec...  10.2 us
  transfers between devices with their start and end apart: 2, of which 2 were waited for; matrix products, arithmetic and copies ran while one was open for 8% of the time, Pallas kernels for 0%

commit v1 on v0

v1 whole, which is shorter than its diff:
```python
import jax
import jax.numpy as jnp
from jax import lax
from jax.experimental import pallas as pl
from jax.experimental.pallas import tpu as pltpu
from jax.sharding import PartitionSpec as P

PAIRS = 1830
SLOTS = 2048
NZ, NY, NX, NC = 16, 4, 4, 2
Q = 512
N = 512
SLAB = NZ * NC
CHUNKS = 4
CHUNK = SLAB // CHUNKS
CHUNK_ROWS = CHUNK * 4 * NX * NY
BLOCK = 32
MESH = pl.DeviceIdType.MESH
F32 = jnp.float32
BF16 = jnp.bfloat16


def device(z, y, x, c):
    return {"cd": z * 4 + (y % 2) * 2 + c, "ab": (y // 2) * 4 + x}


def remote(src, dst, send, recv, target):
    return pltpu.make_async_remote_copy(
        src_ref=src, dst_ref=dst, send_sem=send, recv_sem=recv,
        device_id=target, device_id_type=MESH,
    )


def wait_bytes(ref, sem):
    pltpu.make_async_copy(ref, ref, sem).wait()


def offset_of(k):
    odd = k % 2
    return odd * ((k + 1) // 2) + (1 - odd) * ((NZ - k // 2) % NZ)


def kernel(
    amp, ints, bra, ket, place, out,
    every, other, high, low, w_high, w_low, ints_v, part,
    core_out, core_in, y_out, y_keep, y_in, ring_out, ring_a, ring_b,
    sem_ints, s_z, r_own, r_oth, s_y, r_y, s_x, r_x, s_r, r_r,
    s_c, r_c, s_s, r_s, s_a, r_a, s_b, r_b,
):
    cd, ab = lax.axis_index("cd"), lax.axis_index("ab")
    z, c, x = cd // 4, cd % 2, ab % 4
    parity = (cd // 2) % 2
    y = (ab // 4) * 2 + parity

    barrier = pltpu.get_barrier_semaphore()
    greeted = 0
    for k in range(NZ):
        for dc in range(NC):
            if k or dc:
                zz = (z + offset_of(k)) % NZ
                pl.semaphore_signal(barrier, inc=1, device_id=device(zz, y, x, (c + dc) % 2), device_id_type=MESH)
                greeted += 1
    for d in (1, 2, 3):
        pl.semaphore_signal(barrier, inc=1, device_id=device(z, (y + d) % NY, x, c), device_id_type=MESH)
    right, left = device(z, y, (x + 1) % NX, c), device(z, y, (x + 3) % NX, c)
    for target in (right, left):
        pl.semaphore_signal(barrier, inc=1, device_id=target, device_id_type=MESH)
    load = pltpu.make_async_copy(ints, ints_v, sem_ints)
    load.start()
    pl.semaphore_wait(barrier, greeted + 5)

    def slab(zz, half, core):
        return amp.at[:, pl.ds(pl.multiple_of(zz * 2048 + half * 1024 + core * 512, 512), Q)]

    def send_z(k, dc):
        zz, cc = (z + offset_of(k)) % NZ, (c + dc) % 2
        entry, g, target = k * 2 + c, k // (NZ // CHUNKS), device(zz, y, x, cc)
        remote(slab(zz, 1 - parity, cc), other.at[entry], s_z, r_oth.at[g], target).start()
        remote(slab(zz, parity, cc), every.at[x, y, entry], s_z, r_own.at[g], target).start()

    pltpu.make_async_copy(slab(z, 1 - parity, c), other.at[c], r_oth.at[0]).start()
    pltpu.make_async_copy(slab(z, parity, c), every.at[x, y, c], r_own.at[0]).start()
    send_z(0, 1)

    @pl.loop(1, NZ)
    def _(k):
        send_z(k, 0)
        send_z(k, 1)

    load.wait()
    for i in range(4):
        rows = pl.ds(i * 128, 128)
        picked = jnp.where(bra[rows, :] == ket[...], ints_v[rows, :], 0.0)
        turned = picked.T
        top = turned.astype(BF16)
        w_high[:, rows] = top
        w_low[:, rows] = (turned - top.astype(F32)).astype(BF16)

    def span(g):
        return pl.ds(g * CHUNK, CHUNK)

    def step_y(g):
        wait_bytes(every.at[x, y, span(g)], r_own.at[g])
        own = every.at[x, y, span(g)]
        remote(own, own, s_y.at[0], r_y.at[g, 2], device(z, (y + 2) % NY, x, c)).start()
        remote(own, own, s_x, r_x.at[g, 0, 0], right).start()
        remote(own, own, s_x, r_x.at[g, 1, 0], left).start()
        wait_bytes(other.at[span(g)], r_oth.at[g])
        for d in (1, 3):
            remote(
                other.at[span(g)], every.at[x, y, span(g)], s_y.at[0], r_y.at[g, d],
                device(z, (y + d) % NY, x, c),
            ).start()

    def step_x(g):
        for d in (1, 3, 2):
            ref = every.at[x, (y + NY - d) % NY, span(g)]
            wait_bytes(ref, r_y.at[g, d])
            remote(ref, ref, s_x, r_x.at[g, 0, d], right).start()
            remote(ref, ref, s_x, r_x.at[g, 1, d], left).start()

    def step_relay(g):
        for d in (0, 1, 3, 2):
            yy = (y + NY - d) % NY
            from_left, from_right = every.at[(x + 3) % NX, yy, span(g)], every.at[(x + 1) % NX, yy, span(g)]
            if d in (0, 1):
                wait_bytes(from_left, r_x.at[g, 0, d])
                remote(from_left, from_left, s_r, r_r.at[g, d], right).start()
            else:
                wait_bytes(from_right, r_x.at[g, 1, d])
                remote(from_right, from_right, s_r, r_r.at[g, d], left).start()

    def step_dot(g):
        for d in (0, 1, 3, 2):
            yy = (y + NY - d) % NY
            from_left, from_right = every.at[(x + 3) % NX, yy, span(g)], every.at[(x + 1) % NX, yy, span(g)]
            if d in (0, 1):
                wait_bytes(from_right, r_x.at[g, 1, d])
            else:
                wait_bytes(from_left, r_x.at[g, 0, d])
            wait_bytes(every.at[(x + 2) % NX, yy, span(g)], r_r.at[g, d])

        for xx in range(NX):
            for yy in range(NY):
                value = every[xx, yy, g * CHUNK:(g + 1) * CHUNK].reshape(CHUNK * 4, Q)
                top = value.astype(BF16)
                rows = pl.ds((xx * NY + yy) * CHUNK * 4, CHUNK * 4)
                high[rows, :] = top
                low[rows, :] = (value - top.astype(F32)).astype(BF16)
        for i in range(0, CHUNK_ROWS, 256):
            rows = pl.ds(i, 256)
            result = jnp.dot(high[rows, :], w_high[...], preferred_element_type=F32)
            result += jnp.dot(high[rows, :], w_low[...], preferred_element_type=F32)
            result += jnp.dot(low[rows, :], w_high[...], preferred_element_type=F32)
            part[pl.ds(g * CHUNK_ROWS + i, 256)] = result.reshape(256, 4, 128)

    for t in range(CHUNKS + 3):
        if t < CHUNKS:
            step_y(t)
        if 1 <= t < CHUNKS + 1:
            step_x(t - 1)
        if 2 <= t < CHUNKS + 2:
            step_relay(t - 2)
        if t >= 3:
            step_dot(t - 3)

    def target_z(t):
        return (z + (8 - t // 2 if t % 2 == 0 else 9 + t // 2) % NZ) % NZ if t < 15 else z

    def gather(t, half, core, use):
        base = target_z(t) * 128 + half * 64 + core * 32

        @pl.loop(0, BLOCK, unroll=8)
        def _(i):
            use(i, part[place[base + i]])

    partner_core = device(z, y, x, 1 - c)
    partner_y = device(z, y + 1 - 2 * parity, x, c)
    up, down = device((z + 1) % NZ, y, x, c), device((z + NZ - 1) % NZ, y, x, c)

    def step_gather(t):
        for half in range(2):
            def put(i, row):
                core_out[t, half, i] = row
            gather(t, half, 1 - c, put)
        remote(core_out.at[t], core_in.at[t], s_c, r_c.at[t], partner_core).start()

    def step_core(t):
        wait_bytes(core_in.at[t], r_c.at[t])

        def put_out(i, row):
            y_out[t, i] = row + core_in[t, 1 - parity, i]
        gather(t, 1 - parity, c, put_out)
        remote(y_out.at[t], y_in.at[t], s_s, r_s.at[t], partner_y).start()

        def put_keep(i, row):
            y_keep[t, i] = row + core_in[t, parity, i]
        gather(t, parity, c, put_keep)

    def step_ring(t):
        s = t // 2
        wait_bytes(y_in.at[t], r_s.at[t])
        value = y_keep[t] + y_in[t]
        if t == 15:
            wait_bytes(ring_a.at[7], r_a.at[7])
            wait_bytes(ring_b.at[6], r_b.at[6])
            value = value + ring_a[7] + ring_b[6]
            row = lax.broadcasted_iota(jnp.int32, (BLOCK, 4, 128), 0) + cd * BLOCK
            out[...] = jnp.where(row < PAIRS, value, 0.0)
        elif t % 2 == 0:
            if s:
                wait_bytes(ring_a.at[s - 1], r_a.at[s - 1])
                value = value + ring_a[s - 1]
            ring_out[t] = value
            remote(ring_out.at[t], ring_a.at[s], s_a, r_a.at[s], up).start()
        else:
            if s:
                wait_bytes(ring_b.at[s - 1], r_b.at[s - 1])
                value = value + ring_b[s - 1]
            ring_out[t] = value
            remote(ring_out.at[t], ring_b.at[s], s_b, r_b.at[s], down).start()

    for t in range(16 + 4):
        if t < 16:
            step_gather(t)
        if 1 <= t < 17:
            step_core(t - 1)
        if t >= 4:
            step_ring(t - 4)

    wait_bytes(every.at[0, 0, pl.ds(0, 31)], s_z)
    wait_bytes(every.at[0, 0, pl.ds(0, 31)], s_z)
    for d in range(3):
        wait_bytes(every.at[0, d], s_y.at[0])
    wait_bytes(every.at[0], s_x)
    wait_bytes(every.at[0], s_x)
    wait_bytes(every.at[0], s_r)
    wait_bytes(core_in, s_c)
    wait_bytes(y_in, s_s)
    wait_bytes(ring_a, s_a)
    wait_bytes(ring_b, s_b)


def on_device(amplitudes, integrals, orbital_irrep, bra_pairs, ket_pairs, slot_pair):
    bra = jnp.bitwise_xor(orbital_irrep[bra_pairs[0]], orbital_irrep[bra_pairs[1]])
    ket = jnp.bitwise_xor(orbital_irrep[ket_pairs[0]], orbital_irrep[ket_pairs[1]])
    slot = jnp.arange(SLOTS, dtype=jnp.int32)
    src_ab, src_cd = slot // 4 % 8, slot // 32
    src_x, src_y = src_ab % 4, src_ab // 4 * 2 + src_cd // 2 % 2
    dz = (lax.axis_index("cd") // 4 - src_cd // 4) % NZ
    k = jnp.where(dz == 0, 0, jnp.where(dz <= 8, 2 * dz - 1, 2 * (NZ - dz)))
    entry = k * 2 + src_cd % 2
    spot = (
        entry // CHUNK * CHUNK_ROWS
        + ((src_x * NY + src_y) * CHUNK + entry % CHUNK) * 4
        + slot % 4
    )
    place = jnp.sum(
        jnp.where(slot_pair[None, :] == slot[:, None], spot[None, :], 0), axis=1
    ).astype(jnp.int32)

    dma = pltpu.SemaphoreType.DMA
    result = pl.pallas_call(
        kernel,
        out_shape=jax.ShapeDtypeStruct((BLOCK, 4, 128), F32),
        in_specs=[
            pl.BlockSpec(memory_space=pl.ANY),
            pl.BlockSpec(memory_space=pl.ANY),
            pl.BlockSpec(memory_space=pltpu.VMEM),
            pl.BlockSpec(memory_space=pltpu.VMEM),
            pl.BlockSpec(memory_space=pltpu.SMEM),
        ],
        out_specs=pl.BlockSpec(memory_space=pltpu.VMEM),
        scratch_shapes=[
            pltpu.VMEM((NX, NY, SLAB, 4, Q), F32),
            pltpu.VMEM((SLAB, 4, Q), F32),
            pltpu.VMEM((CHUNK_ROWS, Q), BF16),
            pltpu.VMEM((CHUNK_ROWS, Q), BF16),
            pltpu.VMEM((Q, N), BF16),
            pltpu.VMEM((Q, N), BF16),
            pltpu.VMEM((N, Q), F32),
            pltpu.VMEM((SLOTS, 4, 128), F32),
            pltpu.VMEM((16, 2, BLOCK, 4, 128), F32),
            pltpu.VMEM((16, 2, BLOCK, 4, 128), F32),
            pltpu.VMEM((16, BLOCK, 4, 128), F32),
            pltpu.VMEM((16, BLOCK, 4, 128), F32),
            pltpu.VMEM((16, BLOCK, 4, 128), F32),
            pltpu.VMEM((15, BLOCK, 4, 128), F32),
            pltpu.VMEM((8, BLOCK, 4, 128), F32),
            pltpu.VMEM((7, BLOCK, 4, 128), F32),
            dma,
            dma, dma((CHUNKS,)), dma((CHUNKS,)),
            dma((1,)), dma((CHUNKS, 4)),
            dma, dma((CHUNKS, 2, 4)),
            dma, dma((CHUNKS, 4)),
            dma, dma((16,)),
            dma, dma((16,)),
            dma, dma((8,)),
            dma, dma((7,)),
        ],
        compiler_params=pltpu.CompilerParams(
            collective_id=0, has_side_effects=True, vmem_limit_bytes=48 << 20
        ),
        name="ladder",
    )(amplitudes, integrals, bra[:, None], ket[None, :], place)
    return result.reshape(BLOCK, N)


def solution(mesh):
    in_specs = (P(("cd", "ab"), None), P("ab", "cd"), P(), P(None, "ab"), P(None, "cd"), P())
    out_specs = P("cd", "ab")
    return jax.shard_map(
        on_device, mesh=mesh, in_specs=in_specs, out_specs=out_specs, check_vma=False
    )
```

time: 406 us -> 121 us (0.30)
  the two profiles are of different devices: /device:TPU:2 before, /device:TPU:16 now
where the time goes in v1:
time: 121 us; the launch traced here: 120 us
  Pallas kernels  104 us (86%)
  local copies, waits for them, and re-layouts  13.4 us (11%)
  other arithmetic  2.59 us (2%)
    pallas_call x1, Pallas kernels, on_device(): pl.pallas_call(kernel, out_shape=jax.ShapeDtypeStruct((BLOCK, 4, 128), F3...  104 us
    gather x1, local copies, waits for them, and re-layouts, on_device(): orbital_irrep[ket_pairs[0]]  3.14 us
    gather x1, local copies, waits for them, and re-layouts, on_device(): orbital_irrep[ket_pairs[1]]  3.14 us
    gather x1, local copies, waits for them, and re-layouts, on_device(): orbital_irrep[bra_pairs[0]]  3.14 us
    gather x1, local copies, waits for them, and re-layouts, on_device(): orbital_irrep[bra_pairs[1]]  3.14 us

profile of v1, /device:TPU:16, one launch (start us, length us, event | category | flops | bytes accessed | tf_op | source)
XLA Modules:
  0.0 120.5 jit_solution(6250100153123338405)
XLA Ops:
  0.0 0.0 copy-start
  0.0 0.8 compare_select_fusion.2
  0.8 0.0 copy-done
  0.8 3.1 %gather_fusion = s32[512]{0:T(512)S(1)} fusion(s32[1600]{0:T(1024)S(1)} %copy-done, s32[1024]{0:T(1024)S(1)} %pad_clamp_fusion.3), kind=kCustom, calls=%fused_computation | custom fusion | bytes 6144 | tf_op jit(solution)/shard_map/gather | solution.py:245
  4.0 0.0 copy-start.3
  4.0 3.1 %gather_fusion.1 = s32[512]{0:T(512)S(1)} fusion(s32[1600]{0:T(1024)S(1)} %copy-done, s32[1024]{0:T(1024)S(1)} %pad_clamp_fusion.2), kind=kCustom, calls=%fused_computation.1 | custom fusion | bytes 6144 | tf_op jit(solution)/shard_map/gather | solution.py:245
  7.1 0.0 copy-done.3
  7.2 3.1 %gather_fusion.2 = s32[512]{0:T(512)S(1)} fusion(s32[1600]{0:T(1024)S(1)} %copy-done, s32[1024]{0:T(1024)S(1)} %pad_clamp_fusion.1), kind=kCustom, calls=%fused_computation.2 | custom fusion | bytes 6144 | tf_op jit(solution)/shard_map/gather | solution.py:246
  10.3 0.0 copy-start.4
  10.3 0.0 copy-start.1
  10.4 0.0 copy-start.2
  10.4 3.1 %gather_fusion.3 = s32[512]{0:T(512)S(1)} fusion(s32[1600]{0:T(1024)S(1)} %copy-done, s32[1024]{0:T(1024)S(1)} %pad_clamp_fusion), kind=kCustom, calls=%fused_computation.3 | custom fusion | bytes 6144 | tf_op jit(solution)/shard_map/gather | solution.py:246
  13.6 0.0 copy-done.4
  13.6 1.7 %select_reduce_fusion.place = s32[2048]{0:T(1024)S(1)} fusion(s32[2048]{0:T(1024)S(1)} %fusion.10, s32[2048]{0:T(1024)S(1)} %copy-done.4), kind=kLoop, calls=%fused_computation.4 | loop fusion | flops 12580864 | bytes 24576 | tf_op jit(solution)/shard_map/reduce_sum | solution.py:258
  15.3 0.1 copy.8.bra
  15.5 0.0 copy-done.1
  15.5 0.0 copy-done.2
  15.5 104.4 %ladder.1 = f32[32,4,128]{2,1,0:T(4,128)S(1)} custom-call(f32[4,32768]{1,0:T(4,128)S(1)} %copy-done.2, f32[512,512]{1,0:T(8,128)S(1)} %copy-done.1, s32[512,1]{1,0:T(8,128)S(1)} %copy.8.bra, s32[1,512]{1,0:T(1,128)S(1)} %bitcast.19, s32[2048]{0:T(1024)S(1)} %select_reduce_fusion.place), custom_call_target="tpu_custom_call" | custom-call | tf_op jit(solution)/shard_map/ladder/pallas_call | solution.py:263
  119.9 0.6 copy.11
  (8 shorter events, 0.1 us)
Async XLA Ops:
  0.0 0.8 copy-start
  4.0 3.2 %copy-start.3 = (s32[2,512]{1,0:T(2,128)S(1)}, s32[2,512]{1,0:T(2,128)}, u32[]{:S(2)}) copy-start(s32[2,512]{1,0:T(2,128)} %param.10) | copy-start | bytes 12292
  10.3 3.2 %copy-start.4 = (s32[2048]{0:T(1024)S(1)}, s32[2048]{0:T(1024)}, u32[]{:S(2)}) copy-start(s32[2048]{0:T(1024)} %param.11) | copy-start | bytes 24580
  10.3 5.1 %copy-start.1 = (f32[512,512]{1,0:T(8,128)S(1)}, f32[512,512]{1,0:T(8,128)}, u32[]{:S(2)}) copy-start(f32[512,512]{1,0:T(8,128)} %ints.1) | copy-start | bytes 3145732
  10.4 5.1 %copy-start.2 = (f32[4,32768]{1,0:T(4,128)S(1)}, f32[4,32768]{1,0:T(4,128)}, u32[]{:S(2)}) copy-start(f32[4,32768]{1,0:T(4,128)} %amp.1) | copy-start | bytes 1572868

commit v2 on v1

v2 whole, which is shorter than its diff:
```python
import jax
import jax.numpy as jnp
from jax import lax
from jax.experimental import pallas as pl
from jax.experimental.pallas import tpu as pltpu
from jax.sharding import PartitionSpec as P

PAIRS = 1830
SLOTS = 2048
NZ, NY, NX, NC = 16, 4, 4, 2
Q = 512
N = 512
SLAB = NZ * NC
CHUNKS = 8
STEPS = NZ // CHUNKS
CHUNK = SLAB // CHUNKS
CHUNK_ROWS = CHUNK * 4 * NX * NY
TABLE = 13
BLOCK = 32
ORDER = (
    ("select", 0), ("own", 0), ("oth", 0), ("own", 1), ("oth", 1), ("ownL", 0), ("ownR", 0), ("othL", 0),
    ("othR", 0), ("yown", 0), ("ownL", 1), ("ownR", 1), ("own", 2), ("oth", 2), ("othL", 1), ("othR", 1),
    ("yown", 1), ("oth2", 0), ("d2L", 0), ("place", 0), ("d2R", 0), ("own", 3), ("oth", 3), ("ownR", 2),
    ("ownL", 2), ("othR", 2), ("yown", 2), ("othL", 2), ("d2R", 1), ("oth2", 1), ("d2L", 1), ("own", 4),
    ("oth", 4), ("ownL", 3), ("ownR", 3), ("othL", 3), ("yown", 3), ("othR", 3), ("oth2", 2), ("d2L", 2),
    ("dot", 0), ("d2R", 2), ("ownL", 4), ("own", 5), ("oth", 5), ("othL", 4), ("ownR", 4), ("yown", 4),
    ("othR", 4), ("oth2", 3), ("d2R", 3), ("d2L", 3), ("dot", 1), ("own", 6), ("oth", 6), ("ownR", 5),
    ("ownL", 5), ("othR", 5), ("othL", 5), ("yown", 5), ("d2R", 4), ("d2L", 4), ("own", 7), ("oth", 7),
    ("oth2", 4), ("ownL", 6), ("othL", 6), ("ownR", 6), ("dot", 2), ("othR", 6), ("oth2", 5), ("yown", 6),
    ("d2R", 5), ("d2L", 5), ("dot", 3), ("ownL", 7), ("ownR", 7), ("othL", 7), ("othR", 7), ("yown", 7),
    ("oth2", 6), ("d2L", 6), ("d2R", 6), ("dot", 4), ("oth2", 7), ("d2R", 7), ("dot", 5), ("d2L", 7),
    ("dot", 6), ("dot", 7),
)
MESH = pl.DeviceIdType.MESH
F32 = jnp.float32
BF16 = jnp.bfloat16


def device(z, y, x, c):
    return {"cd": z * 4 + (y % 2) * 2 + c, "ab": (y // 2) * 4 + x}


def remote(src, dst, send, recv, target):
    return pltpu.make_async_remote_copy(
        src_ref=src, dst_ref=dst, send_sem=send, recv_sem=recv,
        device_id=target, device_id_type=MESH,
    )


def wait_bytes(ref, sem):
    pltpu.make_async_copy(ref, ref, sem).wait()


def offset_of(k):
    odd = k % 2
    return odd * ((k + 1) // 2) + (1 - odd) * ((NZ - k // 2) % NZ)


def kernel(
    amp, ints, table, bra, ket, slots, out,
    every, other, high, low, w_high, w_low, ints_v, part, place_v, place,
    core_out, core_in, y_out, y_keep, y_in, ring_out, ring_a, ring_b,
    sem_ints, sem_place, s_z, r_own, r_oth, s_w, s_y, r_y, s_x, r_x, r_ox, s_r, r_r, r_ro,
    s_c, r_c, s_s, r_s, s_a, r_a, s_b, r_b,
):
    cd, ab = lax.axis_index("cd"), lax.axis_index("ab")
    z, c, x = cd // 4, cd % 2, ab % 4
    parity = (cd // 2) % 2
    y = (ab // 4) * 2 + parity

    barrier = pltpu.get_barrier_semaphore()
    greeted = 0
    for k in range(NZ):
        for dc in range(NC):
            if k or dc:
                zz = (z + offset_of(k)) % NZ
                pl.semaphore_signal(barrier, inc=1, device_id=device(zz, y, x, (c + dc) % 2), device_id_type=MESH)
                greeted += 1
    for d in (1, 2, 3):
        pl.semaphore_signal(barrier, inc=1, device_id=device(z, (y + d) % NY, x, c), device_id_type=MESH)
    right, left = device(z, y, (x + 1) % NX, c), device(z, y, (x + 3) % NX, c)
    for target in (right, left):
        pl.semaphore_signal(barrier, inc=1, device_id=target, device_id_type=MESH)
    load = pltpu.make_async_copy(ints, ints_v, sem_ints)
    load.start()
    pl.semaphore_wait(barrier, greeted + 5)

    def slab(zz, half, core):
        return amp.at[:, pl.ds(pl.multiple_of(zz * 2048 + half * 1024 + core * 512, 512), Q)]

    def send_z(k, dc):
        zz, cc = (z + offset_of(k)) % NZ, (c + dc) % 2
        entry, g, target = k * 2 + c, k // STEPS, device(zz, y, x, cc)
        remote(slab(zz, 1 - parity, cc), other.at[x, entry], s_z, r_oth.at[g], target).start()
        remote(slab(zz, parity, cc), every.at[x, y, entry], s_z, r_own.at[g], target).start()

    pltpu.make_async_copy(slab(z, 1 - parity, c), other.at[x, c], r_oth.at[0]).start()
    pltpu.make_async_copy(slab(z, parity, c), every.at[x, y, c], r_own.at[0]).start()
    send_z(0, 1)

    @pl.loop(1, NZ)
    def _(k):
        send_z(k, 0)
        send_z(k, 1)

    def irreps(pairs):
        index = jnp.concatenate([pairs[:, i * 128:(i + 1) * 128] for i in range(4)], axis=0)
        found = jnp.zeros((8, 128), jnp.int32)
        for i in range(TABLE):
            row = jnp.broadcast_to(table[i:i + 1, :], (8, 128))
            value = jnp.take_along_axis(row, index & 127, axis=1, mode="promise_in_bounds")
            found = jnp.where(index >> 7 == i, value, found)
        return [
            (found[2 * i:2 * i + 1] ^ found[2 * i + 1:2 * i + 2]).astype(F32) for i in range(4)
        ]

    def column(row):
        return jnp.broadcast_to(row, (128, 128)).T

    def select_integrals():
        bras, kets = irreps(bra), irreps(ket)
        load.wait()
        for i in range(4):
            bra_irrep = column(bras[i])
            for j in range(4):
                p, q = pl.ds(i * 128, 128), pl.ds(j * 128, 128)
                turned = jnp.where(bra_irrep == kets[j], ints_v[p, q], 0.0).T
                top = turned.astype(BF16)
                w_high[q, p] = top
                w_low[q, p] = (turned - top.astype(F32)).astype(BF16)

    def place_rows():
        place_v[...] = jnp.zeros((16, 128), jnp.int32)
        u = lax.broadcasted_iota(jnp.int32, (128, 128), 0)
        lane = lax.broadcasted_iota(jnp.int32, (128, 128), 1)
        src_x, src_y, src_c = (u >> 2) & 3, ((u >> 4) & 1) * 2 + (u >> 6), (u >> 5) & 1
        fixed = ((src_x * NY + src_y) * CHUNK + src_c) * 4 + (u & 3)

        @pl.loop(0, NZ)
        def _(j):
            dz = (z + NZ - j) % NZ
            k = jnp.where(dz == 0, 0, jnp.where(dz <= 8, 2 * dz - 1, 2 * (NZ - dz)))
            spot = fixed + (k // STEPS * CHUNK_ROWS + k % STEPS * 8)
            pair = column(slots[pl.ds(j, 1), :].astype(F32)).astype(jnp.int32)
            for i in range(16):
                hit = jnp.where(pair == lane + i * 128, spot, 0)
                place_v[i:i + 1, :] += jnp.sum(hit, axis=0, keepdims=True)

        copy = pltpu.make_async_copy(place_v, place, sem_place)
        copy.start()
        copy.wait()

    def span(g):
        return pl.ds(g * CHUNK, CHUNK)

    def row_y(d):
        return (y + NY - d) % NY

    def row_x(d):
        return (x + d) % NX

    def send_x(ref, sems):
        remote(ref, ref, s_x, sems[0], right).start()
        remote(ref, ref, s_x, sems[1], left).start()

    def relay(ref, sem, target):
        remote(ref, ref, s_r, sem, target).start()

    def send_y(g, col):
        for d in (1, 3):
            remote(
                other.at[row_x(col), span(g)], every.at[row_x(col), y, span(g)], s_y,
                r_y.at[g, col, d], device(z, (y + d) % NY, x, c),
            ).start()

    def step_own(g):
        ref = every.at[x, y, span(g)]
        wait_bytes(ref, r_own.at[g])
        remote(ref, ref, s_w, r_y.at[g, 0, 2], device(z, (y + 2) % NY, x, c)).start()
        send_x(ref, (r_x.at[g, 0, 0], r_x.at[g, 1, 0]))

    def step_oth(g):
        ref = other.at[x, span(g)]
        wait_bytes(ref, r_oth.at[g])
        send_x(ref, (r_ox.at[g, 0], r_ox.at[g, 1]))
        send_y(g, 0)

    def step_yown(g):
        ref = every.at[x, row_y(2), span(g)]
        wait_bytes(ref, r_y.at[g, 0, 2])
        send_x(ref, (r_x.at[g, 0, 2], r_x.at[g, 1, 2]))

    def step_ownl(g):
        ref = every.at[row_x(3), y, span(g)]
        wait_bytes(ref, r_x.at[g, 0, 0])
        relay(ref, r_r.at[g, 0], right)

    def step_ownr(g):
        wait_bytes(every.at[row_x(1), y, span(g)], r_x.at[g, 1, 0])

    def step_d2l(g):
        wait_bytes(every.at[row_x(3), row_y(2), span(g)], r_x.at[g, 0, 2])

    def step_d2r(g):
        ref = every.at[row_x(1), row_y(2), span(g)]
        wait_bytes(ref, r_x.at[g, 1, 2])
        relay(ref, r_r.at[g, 2], left)

    def step_othl(g):
        ref = other.at[row_x(3), span(g)]
        wait_bytes(ref, r_ox.at[g, 0])
        if g % 2:
            relay(ref, r_ro.at[g], right)
        send_y(g, 3)

    def step_othr(g):
        ref = other.at[row_x(1), span(g)]
        wait_bytes(ref, r_ox.at[g, 1])
        if g % 2 == 0:
            relay(ref, r_ro.at[g], left)
        send_y(g, 1)

    def step_oth2(g):
        wait_bytes(other.at[row_x(2), span(g)], r_ro.at[g])
        send_y(g, 2)

    def step_dot(g):
        for d in (0, 2):
            wait_bytes(every.at[row_x(2), row_y(d), span(g)], r_r.at[g, d])
        for col in (0, 1, 3, 2):
            for d in (1, 3):
                wait_bytes(every.at[row_x(col), row_y(d), span(g)], r_y.at[g, col, d])

        for xx in range(NX):
            for yy in range(NY):
                value = every[xx, yy, g * CHUNK:(g + 1) * CHUNK].reshape(CHUNK * 4, Q)
                top = value.astype(BF16)
                rows = pl.ds((xx * NY + yy) * CHUNK * 4, CHUNK * 4)
                high[rows, :] = top
                low[rows, :] = (value - top.astype(F32)).astype(BF16)
        result = jnp.dot(high[...], w_high[...], preferred_element_type=F32)
        result += jnp.dot(high[...], w_low[...], preferred_element_type=F32)
        result += jnp.dot(low[...], w_high[...], preferred_element_type=F32)
        part[pl.ds(g * CHUNK_ROWS, CHUNK_ROWS)] = result.reshape(CHUNK_ROWS, 4, 128)

    steps = {
        "own": step_own, "oth": step_oth, "yown": step_yown, "ownL": step_ownl, "ownR": step_ownr,
        "d2L": step_d2l, "d2R": step_d2r, "othL": step_othl, "othR": step_othr, "oth2": step_oth2,
        "dot": step_dot,
    }
    for name, g in ORDER:
        if name == "select":
            select_integrals()
        elif name == "place":
            place_rows()
        else:
            steps[name](g)

    def target_z(t):
        return (z + (8 - t // 2 if t % 2 == 0 else 9 + t // 2) % NZ) % NZ if t < 15 else z

    def gather(t, half, core, use):
        base = target_z(t) * 128 + half * 64 + core * 32

        @pl.loop(0, BLOCK, unroll=8)
        def _(i):
            use(i, part[place[base // 128, base % 128 + i]])

    partner_core = device(z, y, x, 1 - c)
    partner_y = device(z, y + 1 - 2 * parity, x, c)
    up, down = device((z + 1) % NZ, y, x, c), device((z + NZ - 1) % NZ, y, x, c)

    def step_gather(t):
        for half in range(2):
            def put(i, row):
                core_out[t, half, i] = row
            gather(t, half, 1 - c, put)
        remote(core_out.at[t], core_in.at[t], s_c, r_c.at[t], partner_core).start()

    def step_core(t):
        wait_bytes(core_in.at[t], r_c.at[t])

        def put_out(i, row):
            y_out[t, i] = row + core_in[t, 1 - parity, i]
        gather(t, 1 - parity, c, put_out)
        remote(y_out.at[t], y_in.at[t], s_s, r_s.at[t], partner_y).start()

        def put_keep(i, row):
            y_keep[t, i] = row + core_in[t, parity, i]
        gather(t, parity, c, put_keep)

    def step_ring(t):
        s = t // 2
        wait_bytes(y_in.at[t], r_s.at[t])
        value = y_keep[t] + y_in[t]
        if t == 15:
            wait_bytes(ring_a.at[7], r_a.at[7])
            wait_bytes(ring_b.at[6], r_b.at[6])
            value = value + ring_a[7] + ring_b[6]
            row = lax.broadcasted_iota(jnp.int32, (BLOCK, 4, 128), 0) + cd * BLOCK
            out[...] = jnp.where(row < PAIRS, value, 0.0)
        elif t % 2 == 0:
            if s:
                wait_bytes(ring_a.at[s - 1], r_a.at[s - 1])
                value = value + ring_a[s - 1]
            ring_out[t] = value
            remote(ring_out.at[t], ring_a.at[s], s_a, r_a.at[s], up).start()
        else:
            if s:
                wait_bytes(ring_b.at[s - 1], r_b.at[s - 1])
                value = value + ring_b[s - 1]
            ring_out[t] = value
            remote(ring_out.at[t], ring_b.at[s], s_b, r_b.at[s], down).start()

    for t in range(16 + 4):
        if t < 16:
            step_gather(t)
        if 1 <= t < 17:
            step_core(t - 1)
        if t >= 4:
            step_ring(t - 4)

    wait_bytes(every.at[0, 0, pl.ds(0, 31)], s_z)
    wait_bytes(every.at[0, 0, pl.ds(0, 31)], s_z)
    for sem, units in ((s_w, 1), (s_y, 8), (s_x, 6), (s_r, 3)):
        for _ in range(units):
            wait_bytes(every.at[0, 0], sem)
    wait_bytes(core_in, s_c)
    wait_bytes(y_in, s_s)
    wait_bytes(ring_a, s_a)
    wait_bytes(ring_b, s_b)


def on_device(amplitudes, integrals, orbital_irrep, bra_pairs, ket_pairs, slot_pair):
    table = jnp.pad(orbital_irrep, (0, 16 * 128 - orbital_irrep.shape[0])).reshape(16, 128)
    dma = pltpu.SemaphoreType.DMA
    result = pl.pallas_call(
        kernel,
        out_shape=jax.ShapeDtypeStruct((BLOCK, 4, 128), F32),
        in_specs=[
            pl.BlockSpec(memory_space=pl.ANY),
            pl.BlockSpec(memory_space=pl.ANY),
            pl.BlockSpec(memory_space=pltpu.VMEM),
            pl.BlockSpec(memory_space=pltpu.VMEM),
            pl.BlockSpec(memory_space=pltpu.VMEM),
            pl.BlockSpec(memory_space=pltpu.VMEM),
        ],
        out_specs=pl.BlockSpec(memory_space=pltpu.VMEM),
        scratch_shapes=[
            pltpu.VMEM((NX, NY, SLAB, 4, Q), F32),
            pltpu.VMEM((NX, SLAB, 4, Q), F32),
            pltpu.VMEM((CHUNK_ROWS, Q), BF16),
            pltpu.VMEM((CHUNK_ROWS, Q), BF16),
            pltpu.VMEM((Q, N), BF16),
            pltpu.VMEM((Q, N), BF16),
            pltpu.VMEM((N, Q), F32),
            pltpu.VMEM((SLOTS, 4, 128), F32),
            pltpu.VMEM((16, 128), jnp.int32),
            pltpu.SMEM((16, 128), jnp.int32),
            pltpu.VMEM((16, 2, BLOCK, 4, 128), F32),
            pltpu.VMEM((16, 2, BLOCK, 4, 128), F32),
            pltpu.VMEM((16, BLOCK, 4, 128), F32),
            pltpu.VMEM((16, BLOCK, 4, 128), F32),
            pltpu.VMEM((16, BLOCK, 4, 128), F32),
            pltpu.VMEM((15, BLOCK, 4, 128), F32),
            pltpu.VMEM((8, BLOCK, 4, 128), F32),
            pltpu.VMEM((7, BLOCK, 4, 128), F32),
            dma, dma,
            dma, dma((CHUNKS,)), dma((CHUNKS,)),
            dma, dma, dma((CHUNKS, 4, 4)),
            dma, dma((CHUNKS, 2, 4)), dma((CHUNKS, 2)),
            dma, dma((CHUNKS, 4)), dma((CHUNKS,)),
            dma, dma((16,)),
            dma, dma((16,)),
            dma, dma((8,)),
            dma, dma((7,)),
        ],
        compiler_params=pltpu.CompilerParams(
            collective_id=0, has_side_effects=True, vmem_limit_bytes=48 << 20
        ),
        name="ladder",
    )(amplitudes, integrals, table, bra_pairs, ket_pairs, slot_pair.reshape(16, 128))
    return result.reshape(BLOCK, N)


def solution(mesh):
    in_specs = (P(("cd", "ab"), None), P("ab", "cd"), P(), P(None, "ab"), P(None, "cd"), P())
    out_specs = P("cd", "ab")
    return jax.shard_map(
        on_device, mesh=mesh, in_specs=in_specs, out_specs=out_specs, check_vma=False
    )
```

time: 121 us -> 96.2 us (0.80)
  the two profiles are of different devices: /device:TPU:16 before, /device:TPU:8 now
where the time goes in v2:
time: 96.2 us; the launch traced here: 96 us
  Pallas kernels  92.3 us (96%)
  local copies, waits for them, and re-layouts  3.65 us (4%)
    pallas_call x1, Pallas kernels, on_device(): pl.pallas_call(kernel, out_shape=jax.ShapeDtypeStruct((BLOCK, 4, 128), F3...  92.3 us
    unnamed x11, local copies, waits for them, and re-layouts  2.91 us

profile of v2, /device:TPU:8, one launch (start us, length us, event | category | flops | bytes accessed | tf_op | source)
XLA Modules:
  0.0 96.0 jit_solution(15645536028389654936)
XLA Ops:
  0.0 0.0 copy-start.2
  0.0 0.0 copy-start.3
  0.0 0.0 copy-start.4
  0.0 0.7 pad_bitcast_fusion.table
  0.7 0.0 copy-done.2
  0.8 0.0 copy-done.3
  0.8 0.0 copy-done.4
  0.8 0.0 copy-start
  0.8 1.2 %copy-done = f32[512,512]{1,0:T(8,128)S(1)} copy-done((f32[512,512]{1,0:T(8,128)S(1)}, f32[512,512]{1,0:T(8,128)}, u32[]{:S(2)}) %copy-start) | copy-done | bytes 1048600
  2.0 0.0 copy-start.1
  2.0 1.0 %copy-done.1 = f32[4,32768]{1,0:T(4,128)S(1)} copy-done((f32[4,32768]{1,0:T(4,128)S(1)}, f32[4,32768]{1,0:T(4,128)}, u32[]{:S(2)}) %copy-start.1) | copy-done | bytes 524312
  3.0 92.3 %ladder.1 = f32[32,4,128]{2,1,0:T(4,128)S(1)} custom-call(f32[4,32768]{1,0:T(4,128)S(1)} %copy-done.1, f32[512,512]{1,0:T(8,128)S(1)} %copy-done, s32[16,128]{1,0:T(8,128)S(1)} %pad_bitcast_fusion.table, s32[2,512]{1,0:T(2,128)S(1)} %copy-done.3, s32[2,512]{1,0:T(2,128)S(1)} %copy-done.4, s32[16,128]{1,0:T(8,128)S(1)} %bitcast.8), custom_call_target="tpu_custom_call" | custom-call | tf_op jit(solution)/shard_map/ladder/pallas_call | solution.py:337
  95.4 0.6 copy.9
Async XLA Ops:
  0.0 0.8 copy-start.2
  0.0 0.8 copy-start.3
  0.0 0.8 copy-start.4
  0.8 1.2 %copy-start = (f32[512,512]{1,0:T(8,128)S(1)}, f32[512,512]{1,0:T(8,128)}, u32[]{:S(2)}) copy-start(f32[512,512]{1,0:T(8,128)} %ints.1) | copy-start | bytes 3145732
  2.0 1.0 %copy-start.1 = (f32[4,32768]{1,0:T(4,128)S(1)}, f32[4,32768]{1,0:T(4,128)}, u32[]{:S(2)}) copy-start(f32[4,32768]{1,0:T(4,128)} %amp.1) | copy-start | bytes 1572868

commit v3 on v2

--- a/solution.py
+++ b/solution.py
@@ -31,6 +31,26 @@
     ("oth2", 6), ("d2L", 6), ("d2R", 6), ("dot", 4), ("oth2", 7), ("d2R", 7), ("dot", 5), ("d2L", 7),
     ("dot", 6), ("dot", 7),
 )
+WIDE = 8
+NARROW = BLOCK - WIDE
+PIECES = 2
+PIECE = NARROW // PIECES
+SUMS = (
+    ("gather", 0, 0), ("gather", 1, 0), ("gather", 2, 0), ("gather", 3, 0), ("gather", 4, 0),
+    ("gather", 5, 0), ("gather", 6, 0), ("gather", 7, 0), ("core", 0, 0), ("wide", 0, 0), ("core", 1, 0),
+    ("core", 2, 0), ("wide", 2, 0), ("core", 3, 0), ("wide", 3, 0), ("core", 4, 0), ("wide", 4, 0),
+    ("core", 5, 0), ("core", 6, 0), ("core", 7, 0), ("wide", 7, 0), ("sum", 0, 0), ("wide", 1, 0),
+    ("sum", 0, 1), ("gather", 8, 0), ("gather", 9, 0), ("sum", 2, 0), ("gather", 10, 0), ("sum", 2, 1),
+    ("wide", 6, 0), ("sum", 3, 0), ("gather", 11, 0), ("sum", 3, 1), ("gather", 12, 0), ("sum", 4, 0),
+    ("gather", 13, 0), ("core", 8, 0), ("wide", 8, 0), ("sum", 4, 1), ("core", 9, 0), ("sum", 1, 0),
+    ("core", 10, 0), ("core", 11, 0), ("wide", 11, 0), ("core", 12, 0), ("wide", 12, 0), ("sum", 1, 1),
+    ("wide", 5, 0), ("core", 13, 0), ("sum", 7, 0), ("sum", 7, 1), ("sum", 8, 0), ("sum", 6, 0),
+    ("sum", 8, 1), ("gather", 14, 0), ("wide", 10, 0), ("gather", 15, 0), ("sum", 5, 0), ("sum", 6, 1),
+    ("sum", 11, 0), ("sum", 5, 1), ("core", 14, 0), ("sum", 11, 1), ("core", 15, 0), ("sum", 12, 0),
+    ("sum", 12, 1), ("wide", 9, 0), ("sum", 10, 0), ("wide", 14, 0), ("sum", 9, 0), ("sum", 10, 1),
+    ("sum", 9, 1), ("sum", 14, 0), ("wide", 13, 0), ("sum", 13, 0), ("sum", 14, 1), ("sum", 13, 1),
+    ("wide", 15, 0), ("sum", 15, 0), ("sum", 15, 1),
+)
 MESH = pl.DeviceIdType.MESH
 F32 = jnp.float32
 BF16 = jnp.bfloat16
@@ -59,9 +79,9 @@
 def kernel(
     amp, ints, table, bra, ket, slots, out,
     every, other, high, low, w_high, w_low, ints_v, part, place_v, place,
-    core_out, core_in, y_out, y_keep, y_in, ring_out, ring_a, ring_b,
+    core_out, core_in, y_out, y_keep, y_in, y_last, wide, sum_out, sum_in, wide_out, wide_in,
     sem_ints, sem_place, s_z, r_own, r_oth, s_w, s_y, r_y, s_x, r_x, r_ox, s_r, r_r, r_ro,
-    s_c, r_c, s_s, r_s, s_a, r_a, s_b, r_b,
+    s_c, r_c, s_s, r_s, s_sum, r_sum, s_wide, r_wide, s_last, r_last,
 ):
     cd, ab = lax.axis_index("cd"), lax.axis_index("ab")
     z, c, x = cd // 4, cd % 2, ab % 4
@@ -256,69 +276,105 @@
         else:
             steps[name](g)
 
+    def arm_of(t):
+        return (0, 8) if t == 0 else ((t + 1) % 2, 7 - (t - 1) // 2)
+
     def target_z(t):
-        return (z + (8 - t // 2 if t % 2 == 0 else 9 + t // 2) % NZ) % NZ if t < 15 else z
-
-    def gather(t, half, core, use):
-        base = target_z(t) * 128 + half * 64 + core * 32
-
-        @pl.loop(0, BLOCK, unroll=8)
+        arm, d = arm_of(t)
+        return (z + (NZ - d if arm else d)) % NZ
+
+    def sources(t):
+        arm, d = arm_of(t)
+        if t == 15:
+            return [(0, 1), (1, 1)]
+        top = 7 if arm else 8
+        return [(arm, e) for e in (d + 1, d + 2) if d % 2 and e <= top and (e == d + 1 or e % 2)]
+
+    def receiver(t):
+        arm, d = arm_of(t)
+        hops = 2 if d % 2 and d > 1 else 1
+        return device((z + (NZ - hops if arm else hops)) % NZ, y, x, c)
+
+    def gather(t, half, core, first, count, use):
+        base = target_z(t) * 128 + half * 64 + core * 32 + first
+
+        @pl.loop(0, count, unroll=8)
         def _(i):
             use(i, part[place[base // 128, base % 128 + i]])
 
     partner_core = device(z, y, x, 1 - c)
     partner_y = device(z, y + 1 - 2 * parity, x, c)
-    up, down = device((z + 1) % NZ, y, x, c), device((z + NZ - 1) % NZ, y, x, c)
 
     def step_gather(t):
         for half in range(2):
             def put(i, row):
                 core_out[t, half, i] = row
-            gather(t, half, 1 - c, put)
+            gather(t, half, 1 - c, 0, BLOCK, put)
         remote(core_out.at[t], core_in.at[t], s_c, r_c.at[t], partner_core).start()
+
+    def piece(i):
+        return pl.ds(i * PIECE, PIECE)
 
     def step_core(t):
         wait_bytes(core_in.at[t], r_c.at[t])
 
         def put_out(i, row):
             y_out[t, i] = row + core_in[t, 1 - parity, i]
-        gather(t, 1 - parity, c, put_out)
-        remote(y_out.at[t], y_in.at[t], s_s, r_s.at[t], partner_y).start()
+        gather(t, 1 - parity, c, 0, NARROW, put_out)
+        for i in range(PIECES):
+            remote(y_out.at[t, piece(i)], y_in.at[t, piece(i)], s_s, r_s.at[t, i], partner_y).start()
 
         def put_keep(i, row):
             y_keep[t, i] = row + core_in[t, parity, i]
-        gather(t, parity, c, put_keep)
-
-    def step_ring(t):
-        s = t // 2
-        wait_bytes(y_in.at[t], r_s.at[t])
-        value = y_keep[t] + y_in[t]
+        gather(t, parity, c, 0, NARROW, put_keep)
+        if WIDE:
+            for half in range(2):
+                def put_wide(i, row):
+                    wide[t, half, i] = row + core_in[t, half, NARROW + i]
+                gather(t, half, c, NARROW, WIDE, put_wide)
+
+    def finish(value, first):
+        row = lax.broadcasted_iota(jnp.int32, value.shape, 0) + (cd * BLOCK + first)
+        return jnp.where(row < PAIRS, value, 0.0)
+
+    def step_sum(t, i):
+        rows = piece(i)
+        wait_bytes(y_in.at[t, rows], r_s.at[t, i])
+        value = y_keep[t, rows] + y_in[t, rows]
+        for arm, d in sources(t):
+            wait_bytes(sum_in.at[arm, d - 1, rows], r_sum.at[arm, d - 1, i])
+            value = value + sum_in[arm, d - 1, rows]
         if t == 15:
-            wait_bytes(ring_a.at[7], r_a.at[7])
-            wait_bytes(ring_b.at[6], r_b.at[6])
-            value = value + ring_a[7] + ring_b[6]
-            row = lax.broadcasted_iota(jnp.int32, (BLOCK, 4, 128), 0) + cd * BLOCK
-            out[...] = jnp.where(row < PAIRS, value, 0.0)
-        elif t % 2 == 0:
-            if s:
-                wait_bytes(ring_a.at[s - 1], r_a.at[s - 1])
-                value = value + ring_a[s - 1]
-            ring_out[t] = value
-            remote(ring_out.at[t], ring_a.at[s], s_a, r_a.at[s], up).start()
+            out[rows] = finish(value, i * PIECE)
+            return
+        arm, d = arm_of(t)
+        sum_out[t, rows] = value
+        remote(sum_out.at[t, rows], sum_in.at[arm, d - 1, rows], s_sum, r_sum.at[arm, d - 1, i], receiver(t)).start()
+
+    def step_wide(t):
+        value = wide[t]
+        for arm, d in sources(t):
+            wait_bytes(wide_in.at[arm, d - 1], r_wide.at[arm, d - 1])
+            value = value + wide_in[arm, d - 1]
+        wide_out[t] = value
+        if t == 15:
+            remote(wide_out.at[15, 1 - parity], y_last, s_last, r_last, partner_y).start()
+            return
+        arm, d = arm_of(t)
+        remote(wide_out.at[t], wide_in.at[arm, d - 1], s_wide, r_wide.at[arm, d - 1], receiver(t)).start()
+
+    for name, t, i in SUMS:
+        if name == "gather":
+            step_gather(t)
+        elif name == "core":
+            step_core(t)
+        elif name == "sum":
+            step_sum(t, i)
         else:
-            if s:
-                wait_bytes(ring_b.at[s - 1], r_b.at[s - 1])
-                value = value + ring_b[s - 1]
-            ring_out[t] = value
-            remote(ring_out.at[t], ring_b.at[s], s_b, r_b.at[s], down).start()
-
-    for t in range(16 + 4):
-        if t < 16:
-            step_gather(t)
-        if 1 <= t < 17:
-            step_core(t - 1)
-        if t >= 4:
-            step_ring(t - 4)
+            step_wide(t)
+    if WIDE:
+        wait_bytes(y_last, r_last)
+        out[NARROW:BLOCK] = finish(wide_out[15, parity] + y_last[...], NARROW)
 
     wait_bytes(every.at[0, 0, pl.ds(0, 31)], s_z)
     wait_bytes(every.at[0, 0, pl.ds(0, 31)], s_z)
@@ -327,8 +383,10 @@
             wait_bytes(every.at[0, 0], sem)
     wait_bytes(core_in, s_c)
     wait_bytes(y_in, s_s)
-    wait_bytes(ring_a, s_a)
-    wait_bytes(ring_b, s_b)
+    wait_bytes(sum_out.at[pl.ds(0, 15)], s_sum)
+    if WIDE:
+        wait_bytes(wide_out.at[pl.ds(0, 15)], s_wide)
+        wait_bytes(y_last, s_last)
 
 
 def on_device(amplitudes, integrals, orbital_irrep, bra_pairs, ket_pairs, slot_pair):
@@ -359,24 +417,28 @@
             pltpu.SMEM((16, 128), jnp.int32),
             pltpu.VMEM((16, 2, BLOCK, 4, 128), F32),
             pltpu.VMEM((16, 2, BLOCK, 4, 128), F32),
-            pltpu.VMEM((16, BLOCK, 4, 128), F32),
-            pltpu.VMEM((16, BLOCK, 4, 128), F32),
-            pltpu.VMEM((16, BLOCK, 4, 128), F32),
-            pltpu.VMEM((15, BLOCK, 4, 128), F32),
-            pltpu.VMEM((8, BLOCK, 4, 128), F32),
-            pltpu.VMEM((7, BLOCK, 4, 128), F32),
+            pltpu.VMEM((16, NARROW, 4, 128), F32),
+            pltpu.VMEM((16, NARROW, 4, 128), F32),
+            pltpu.VMEM((16, NARROW, 4, 128), F32),
+            pltpu.VMEM((max(WIDE, 1), 4, 128), F32),
+            pltpu.VMEM((16, 2, max(WIDE, 1), 4, 128), F32),
+            pltpu.VMEM((16, NARROW, 4, 128), F32),
+            pltpu.VMEM((2, 8, NARROW, 4, 128), F32),
+            pltpu.VMEM((16, 2, max(WIDE, 1), 4, 128), F32),
+            pltpu.VMEM((2, 8, 2, max(WIDE, 1), 4, 128), F32),
             dma, dma,
             dma, dma((CHUNKS,)), dma((CHUNKS,)),
             dma, dma, dma((CHUNKS, 4, 4)),
             dma, dma((CHUNKS, 2, 4)), dma((CHUNKS, 2)),
             dma, dma((CHUNKS, 4)), dma((CHUNKS,)),
             dma, dma((16,)),
-            dma, dma((16,)),
-            dma, dma((8,)),
-            dma, dma((7,)),
+            dma, dma((16, PIECES)),
+            dma, dma((2, 8, PIECES)),
+            dma, dma((2, 8)),
+            dma, dma,
         ],
         compiler_params=pltpu.CompilerParams(
-            collective_id=0, has_side_effects=True, vmem_limit_bytes=48 << 20
+            collective_id=0, has_side_effects=True, vmem_limit_bytes=60 << 20
         ),
         name="ladder",
     )(amplitudes, integrals, table, bra_pairs, ket_pairs, slot_pair.reshape(16, 128))

time: 96.2 us -> 93.1 us (0.968)
  Pallas kernels: 92.3 us -> 90.1 us
    pallas_call x1, Pallas kernels: 92.3 us -> 90.1 us  [on_device(): pl.pallas_call(kernel, out_shape=jax.ShapeDtypeStruct((BLOCK, 4, 128), F3...]
    unnamed x11 -> x1, local copies, waits for them, and re-layouts: 2.91 us -> 1.47 us
where the time goes in v3:
time: 93.1 us; the launch traced here: 92.9 us
  Pallas kernels  90.1 us (97%)
  local copies, waits for them, and re-layouts  2.77 us (3%)
    pallas_call x1, Pallas kernels, on_device(): pl.pallas_call(kernel, out_shape=jax.ShapeDtypeStruct((BLOCK, 4, 128), F3...  90.1 us

profile of v3, /device:TPU:8, one launch (start us, length us, event | category | flops | bytes accessed | tf_op | source)
XLA Modules:
  0.0 92.9 jit_solution(8169018239998345766)
XLA Ops:
  0.0 1.3 %pad_bitcast_fusion.table = s32[16,128]{1,0:T(8,128)} fusion(s32[1600]{0:T(1024)} %param.8), kind=kLoop, calls=%fused_computation.1 | loop fusion | bytes 14592 | tf_op jit(solution)/shard_map/reshape | solution.py:393
  1.3 90.1 %ladder.1 = f32[32,4,128]{2,1,0:T(4,128)} custom-call(f32[4,32768]{1,0:T(4,128)} %amp.1, f32[512,512]{1,0:T(8,128)} %ints.1, s32[16,128]{1,0:T(8,128)} %pad_bitcast_fusion.table, s32[2,512]{1,0:T(2,128)} %bra.1, s32[2,512]{1,0:T(2,128)} %ket.1, s32[16,128]{1,0:T(8,128)} %bitcast.8), custom_call_target="tpu_custom_call" | custom-call | tf_op jit(solution)/shard_map/ladder/pallas_call | solution.py:395
  91.4 1.5 %copy.9 = f32[4,8,4,128]{3,1,2,0:T(8,128)} copy(f32[4,8,4,128]{3,2,1,0:T(4,128)} %bitcast.7) | data formatting | bytes 131072

commit v4 on v3

--- a/solution.py
+++ b/solution.py
@@ -18,7 +18,7 @@
 TABLE = 13
 BLOCK = 32
 ORDER = (
-    ("select", 0), ("own", 0), ("oth", 0), ("own", 1), ("oth", 1), ("ownL", 0), ("ownR", 0), ("othL", 0),
+    ("select", 0), ("own", 0), ("oth", 0), ("far", 0), ("own", 1), ("oth", 1), ("ownL", 0), ("ownR", 0), ("othL", 0),
     ("othR", 0), ("yown", 0), ("ownL", 1), ("ownR", 1), ("own", 2), ("oth", 2), ("othL", 1), ("othR", 1),
     ("yown", 1), ("oth2", 0), ("d2L", 0), ("place", 0), ("d2R", 0), ("own", 3), ("oth", 3), ("ownR", 2),
     ("ownL", 2), ("othR", 2), ("yown", 2), ("othL", 2), ("d2R", 1), ("oth2", 1), ("d2L", 1), ("own", 4),
@@ -31,7 +31,7 @@
     ("oth2", 6), ("d2L", 6), ("d2R", 6), ("dot", 4), ("oth2", 7), ("d2R", 7), ("dot", 5), ("d2L", 7),
     ("dot", 6), ("dot", 7),
 )
-WIDE = 8
+WIDE = 4
 NARROW = BLOCK - WIDE
 PIECES = 2
 PIECE = NARROW // PIECES
@@ -39,18 +39,19 @@
     ("gather", 0, 0), ("gather", 1, 0), ("gather", 2, 0), ("gather", 3, 0), ("gather", 4, 0),
     ("gather", 5, 0), ("gather", 6, 0), ("gather", 7, 0), ("core", 0, 0), ("wide", 0, 0), ("core", 1, 0),
     ("core", 2, 0), ("wide", 2, 0), ("core", 3, 0), ("wide", 3, 0), ("core", 4, 0), ("wide", 4, 0),
-    ("core", 5, 0), ("core", 6, 0), ("core", 7, 0), ("wide", 7, 0), ("sum", 0, 0), ("wide", 1, 0),
-    ("sum", 0, 1), ("gather", 8, 0), ("gather", 9, 0), ("sum", 2, 0), ("gather", 10, 0), ("sum", 2, 1),
-    ("wide", 6, 0), ("sum", 3, 0), ("gather", 11, 0), ("sum", 3, 1), ("gather", 12, 0), ("sum", 4, 0),
-    ("gather", 13, 0), ("core", 8, 0), ("wide", 8, 0), ("sum", 4, 1), ("core", 9, 0), ("sum", 1, 0),
-    ("core", 10, 0), ("core", 11, 0), ("wide", 11, 0), ("core", 12, 0), ("wide", 12, 0), ("sum", 1, 1),
-    ("wide", 5, 0), ("core", 13, 0), ("sum", 7, 0), ("sum", 7, 1), ("sum", 8, 0), ("sum", 6, 0),
-    ("sum", 8, 1), ("gather", 14, 0), ("wide", 10, 0), ("gather", 15, 0), ("sum", 5, 0), ("sum", 6, 1),
-    ("sum", 11, 0), ("sum", 5, 1), ("core", 14, 0), ("sum", 11, 1), ("core", 15, 0), ("sum", 12, 0),
-    ("sum", 12, 1), ("wide", 9, 0), ("sum", 10, 0), ("wide", 14, 0), ("sum", 9, 0), ("sum", 10, 1),
-    ("sum", 9, 1), ("sum", 14, 0), ("wide", 13, 0), ("sum", 13, 0), ("sum", 14, 1), ("sum", 13, 1),
-    ("wide", 15, 0), ("sum", 15, 0), ("sum", 15, 1),
+    ("core", 5, 0), ("core", 6, 0), ("core", 7, 0), ("wide", 7, 0), ("wide", 1, 0), ("sum", 0, 0),
+    ("sum", 0, 1), ("gather", 8, 0), ("gather", 9, 0), ("wide", 6, 0), ("sum", 2, 0), ("gather", 10, 0),
+    ("gather", 11, 0), ("sum", 2, 1), ("gather", 12, 0), ("sum", 3, 0), ("gather", 13, 0), ("sum", 3, 1),
+    ("core", 8, 0), ("wide", 8, 0), ("core", 9, 0), ("sum", 4, 0), ("sum", 1, 0), ("wide", 5, 0),
+    ("core", 10, 0), ("sum", 4, 1), ("core", 11, 0), ("wide", 11, 0), ("sum", 1, 1), ("core", 12, 0),
+    ("wide", 12, 0), ("core", 13, 0), ("wide", 10, 0), ("sum", 7, 0), ("gather", 14, 0), ("sum", 6, 0),
+    ("sum", 7, 1), ("gather", 15, 0), ("sum", 6, 1), ("sum", 8, 0), ("sum", 5, 0), ("sum", 8, 1),
+    ("wide", 13, 0), ("wide", 9, 0), ("core", 14, 0), ("wide", 14, 0), ("core", 15, 0), ("sum", 5, 1),
+    ("sum", 11, 0), ("sum", 11, 1), ("sum", 12, 0), ("sum", 9, 0), ("sum", 10, 0), ("sum", 12, 1),
+    ("sum", 10, 1), ("wide", 15, 0), ("sum", 13, 0), ("sum", 9, 1), ("sum", 14, 0), ("sum", 13, 1),
+    ("sum", 14, 1), ("sum", 15, 0), ("sum", 15, 1),
 )
+NEXT = (-1, 0, 1, 0, 3, 3, 5, 5, 7)
 MESH = pl.DeviceIdType.MESH
 F32 = jnp.float32
 BF16 = jnp.bfloat16
@@ -77,10 +78,10 @@
 
 
 def kernel(
-    amp, ints, table, bra, ket, slots, out,
+    amp_hbm, ints, table, bra, ket, slots, out,
     every, other, high, low, w_high, w_low, ints_v, part, place_v, place,
     core_out, core_in, y_out, y_keep, y_in, y_last, wide, sum_out, sum_in, wide_out, wide_in,
-    sem_ints, sem_place, s_z, r_own, r_oth, s_w, s_y, r_y, s_x, r_x, r_ox, s_r, r_r, r_ro,
+    amp, sem_amp, sem_two, sem_four, sem_ints, sem_place, s_z, r_own, r_oth, s_w, s_y, r_y, s_x, r_x, r_ox, s_r, r_r, r_ro,
     s_c, r_c, s_s, r_s, s_sum, r_sum, s_wide, r_wide, s_last, r_last,
 ):
     cd, ab = lax.axis_index("cd"), lax.axis_index("ab")
@@ -89,21 +90,24 @@
     y = (ab // 4) * 2 + parity
 
     barrier = pltpu.get_barrier_semaphore()
-    greeted = 0
-    for k in range(NZ):
-        for dc in range(NC):
-            if k or dc:
-                zz = (z + offset_of(k)) % NZ
-                pl.semaphore_signal(barrier, inc=1, device_id=device(zz, y, x, (c + dc) % 2), device_id_type=MESH)
-                greeted += 1
-    for d in (1, 2, 3):
-        pl.semaphore_signal(barrier, inc=1, device_id=device(z, (y + d) % NY, x, c), device_id_type=MESH)
     right, left = device(z, y, (x + 1) % NX, c), device(z, y, (x + 3) % NX, c)
-    for target in (right, left):
+    greet = [device(z, y, x, 1 - c), right, left]
+    greet += [device(z, (y + d) % NY, x, c) for d in (1, 2, 3)]
+    greet += [device((z + d) % NZ, y, x, (c + dc) % 2) for d in (1, 15, 2, 14) for dc in range(NC)]
+    for target in greet:
         pl.semaphore_signal(barrier, inc=1, device_id=target, device_id_type=MESH)
     load = pltpu.make_async_copy(ints, ints_v, sem_ints)
     load.start()
-    pl.semaphore_wait(barrier, greeted + 5)
+    stage = pltpu.make_async_copy(amp_hbm, amp, sem_amp)
+    stage.start()
+    pl.semaphore_wait(barrier, len(greet))
+
+    def vouch(sem, d):
+        for zz in ((z + d) % NZ, (z + NZ - d) % NZ):
+            pl.semaphore_signal(sem, inc=1, device_id=device(zz, y, x, c), device_id_type=MESH)
+
+    vouch(sem_two, 2)
+    stage.wait()
 
     def slab(zz, half, core):
         return amp.at[:, pl.ds(pl.multiple_of(zz * 2048 + half * 1024 + core * 512, 512), Q)]
@@ -118,16 +122,31 @@
     pltpu.make_async_copy(slab(z, parity, c), every.at[x, y, c], r_own.at[0]).start()
     send_z(0, 1)
 
-    @pl.loop(1, NZ)
-    def _(k):
-        send_z(k, 0)
-        send_z(k, 1)
+    def send_range(first, last):
+        @pl.loop(first, last)
+        def _(k):
+            send_z(k, 0)
+            send_z(k, 1)
+
+    send_range(1, 5)
+    pl.semaphore_wait(sem_two, 2)
+    vouch(sem_four, 4)
+    send_range(5, 9)
+
+    def send_far():
+        pl.semaphore_wait(sem_four, 2)
+        send_range(9, NZ)
 
     def irreps(pairs):
         index = jnp.concatenate([pairs[:, i * 128:(i + 1) * 128] for i in range(4)], axis=0)
         found = jnp.zeros((8, 128), jnp.int32)
         for i in range(TABLE):
-            row = jnp.broadcast_to(table[i:i + 1, :], (8, 128))
+            if (i + 1) * 128 <= table.shape[0]:
+                row = table[pl.ds(i * 128, 128)].reshape(1, 128)
+            else:
+                rest = table[pl.ds(i * 128, table.shape[0] - i * 128)].reshape(1, table.shape[0] - i * 128)
+                row = jnp.concatenate([rest, jnp.zeros((1, 128 - rest.shape[1]), jnp.int32)], axis=1)
+            row = jnp.broadcast_to(row, (8, 128))
             value = jnp.take_along_axis(row, index & 127, axis=1, mode="promise_in_bounds")
             found = jnp.where(index >> 7 == i, value, found)
         return [
@@ -269,7 +288,9 @@
         "dot": step_dot,
     }
     for name, g in ORDER:
-        if name == "select":
+        if name == "far":
+            send_far()
+        elif name == "select":
             select_integrals()
         elif name == "place":
             place_rows()
@@ -285,15 +306,16 @@
 
     def sources(t):
         arm, d = arm_of(t)
-        if t == 15:
-            return [(0, 1), (1, 1)]
-        top = 7 if arm else 8
-        return [(arm, e) for e in (d + 1, d + 2) if d % 2 and e <= top and (e == d + 1 or e % 2)]
+        arms = (0, 1) if t == 15 else (arm,)
+        return [(a, e) for a in arms for e in range(1, 8 if a else 9) if NEXT[e] == d]
 
     def receiver(t):
         arm, d = arm_of(t)
-        hops = 2 if d % 2 and d > 1 else 1
+        hops = d - NEXT[d]
         return device((z + (NZ - hops if arm else hops)) % NZ, y, x, c)
+
+    def holds_rows(t, half):
+        return target_z(t) * 128 + half * 64 < PAIRS
 
     def gather(t, half, core, first, count, use):
         base = target_z(t) * 128 + half * 64 + core * 32 + first
@@ -306,28 +328,35 @@
     partner_y = device(z, y + 1 - 2 * parity, x, c)
 
     def step_gather(t):
-        for half in range(2):
-            def put(i, row):
-                core_out[t, half, i] = row
-            gather(t, half, 1 - c, 0, BLOCK, put)
-        remote(core_out.at[t], core_in.at[t], s_c, r_c.at[t], partner_core).start()
+        @pl.when(holds_rows(t, 0))
+        def _():
+            for half in range(2):
+                def put(i, row):
+                    core_out[t, half, i] = row
+                gather(t, half, 1 - c, 0, BLOCK, put)
+            remote(core_out.at[t], core_in.at[t], s_c, r_c.at[t], partner_core).start()
 
     def piece(i):
         return pl.ds(i * PIECE, PIECE)
 
     def step_core(t):
-        wait_bytes(core_in.at[t], r_c.at[t])
-
-        def put_out(i, row):
-            y_out[t, i] = row + core_in[t, 1 - parity, i]
-        gather(t, 1 - parity, c, 0, NARROW, put_out)
-        for i in range(PIECES):
-            remote(y_out.at[t, piece(i)], y_in.at[t, piece(i)], s_s, r_s.at[t, i], partner_y).start()
-
-        def put_keep(i, row):
-            y_keep[t, i] = row + core_in[t, parity, i]
-        gather(t, parity, c, 0, NARROW, put_keep)
-        if WIDE:
+        @pl.when(holds_rows(t, 0))
+        def _():
+            wait_bytes(core_in.at[t], r_c.at[t])
+
+        @pl.when(holds_rows(t, 1 - parity))
+        def _():
+            def put_out(i, row):
+                y_out[t, i] = row + core_in[t, 1 - parity, i]
+            gather(t, 1 - parity, c, 0, NARROW, put_out)
+            for i in range(PIECES):
+                remote(y_out.at[t, piece(i)], y_in.at[t, piece(i)], s_s, r_s.at[t, i], partner_y).start()
+
+        @pl.when(holds_rows(t, 0))
+        def _():
+            def put_keep(i, row):
+                y_keep[t, i] = row + core_in[t, parity, i]
+            gather(t, parity, c, 0, NARROW, put_keep)
             for half in range(2):
                 def put_wide(i, row):
                     wide[t, half, i] = row + core_in[t, half, NARROW + i]
@@ -339,29 +368,43 @@
 
     def step_sum(t, i):
         rows = piece(i)
-        wait_bytes(y_in.at[t, rows], r_s.at[t, i])
-        value = y_keep[t, rows] + y_in[t, rows]
-        for arm, d in sources(t):
-            wait_bytes(sum_in.at[arm, d - 1, rows], r_sum.at[arm, d - 1, i])
-            value = value + sum_in[arm, d - 1, rows]
-        if t == 15:
-            out[rows] = finish(value, i * PIECE)
-            return
-        arm, d = arm_of(t)
-        sum_out[t, rows] = value
-        remote(sum_out.at[t, rows], sum_in.at[arm, d - 1, rows], s_sum, r_sum.at[arm, d - 1, i], receiver(t)).start()
+
+        @pl.when(holds_rows(t, parity))
+        def _():
+            wait_bytes(y_in.at[t, rows], r_s.at[t, i])
+            value = y_keep[t, rows] + y_in[t, rows]
+            for arm, d in sources(t):
+                wait_bytes(sum_in.at[arm, d - 1, rows], r_sum.at[arm, d - 1, i])
+                value = value + sum_in[arm, d - 1, rows]
+            if t == 15:
+                out[rows] = finish(value, i * PIECE)
+                return
+            arm, d = arm_of(t)
+            sum_out[t, rows] = value
+            remote(
+                sum_out.at[t, rows], sum_in.at[arm, d - 1, rows], s_sum,
+                r_sum.at[arm, d - 1, i], receiver(t),
+            ).start()
 
     def step_wide(t):
-        value = wide[t]
-        for arm, d in sources(t):
-            wait_bytes(wide_in.at[arm, d - 1], r_wide.at[arm, d - 1])
-            value = value + wide_in[arm, d - 1]
-        wide_out[t] = value
-        if t == 15:
-            remote(wide_out.at[15, 1 - parity], y_last, s_last, r_last, partner_y).start()
-            return
-        arm, d = arm_of(t)
-        remote(wide_out.at[t], wide_in.at[arm, d - 1], s_wide, r_wide.at[arm, d - 1], receiver(t)).start()
+        @pl.when(holds_rows(t, 0))
+        def _():
+            value = wide[t]
+            for arm, d in sources(t):
+                wait_bytes(wide_in.at[arm, d - 1], r_wide.at[arm, d - 1])
+                value = value + wide_in[arm, d - 1]
+            wide_out[t] = value
+            if t == 15:
+                remote(wide_out.at[15, 1 - parity], y_last, s_last, r_last, partner_y).start()
+                return
+            arm, d = arm_of(t)
+            remote(
+                wide_out.at[t], wide_in.at[arm, d - 1], s_wide, r_wide.at[arm, d - 1], receiver(t)
+            ).start()
+
+    @pl.when(cd * BLOCK >= PAIRS)
+    def _():
+        out[...] = jnp.zeros(out.shape, F32)
 
     for name, t, i in SUMS:
         if name == "gather":
@@ -372,7 +415,9 @@
             step_sum(t, i)
         else:
             step_wide(t)
-    if WIDE:
+
+    @pl.when(holds_rows(15, 0))
+    def _():
         wait_bytes(y_last, r_last)
         out[NARROW:BLOCK] = finish(wide_out[15, parity] + y_last[...], NARROW)
 
@@ -381,16 +426,23 @@
     for sem, units in ((s_w, 1), (s_y, 8), (s_x, 6), (s_r, 3)):
         for _ in range(units):
             wait_bytes(every.at[0, 0], sem)
-    wait_bytes(core_in, s_c)
-    wait_bytes(y_in, s_s)
-    wait_bytes(sum_out.at[pl.ds(0, 15)], s_sum)
-    if WIDE:
-        wait_bytes(wide_out.at[pl.ds(0, 15)], s_wide)
-        wait_bytes(y_last, s_last)
+    for t in range(16):
+        @pl.when(holds_rows(t, 0))
+        def _():
+            wait_bytes(core_in.at[t], s_c)
+            wait_bytes(wide_out.at[t] if t < 15 else y_last, s_wide if t < 15 else s_last)
+
+        @pl.when(holds_rows(t, 1 - parity))
+        def _():
+            wait_bytes(y_in.at[t], s_s)
+
+        if t < 15:
+            @pl.when(holds_rows(t, parity))
+            def _():
+                wait_bytes(sum_out.at[t], s_sum)
 
 
 def on_device(amplitudes, integrals, orbital_irrep, bra_pairs, ket_pairs, slot_pair):
-    table = jnp.pad(orbital_irrep, (0, 16 * 128 - orbital_irrep.shape[0])).reshape(16, 128)
     dma = pltpu.SemaphoreType.DMA
     result = pl.pallas_call(
         kernel,
@@ -426,6 +478,8 @@
             pltpu.VMEM((2, 8, NARROW, 4, 128), F32),
             pltpu.VMEM((16, 2, max(WIDE, 1), 4, 128), F32),
             pltpu.VMEM((2, 8, 2, max(WIDE, 1), 4, 128), F32),
+            pltpu.VMEM((4, NZ * 2048), F32), dma,
+            pltpu.SemaphoreType.REGULAR, pltpu.SemaphoreType.REGULAR,
             dma, dma,
             dma, dma((CHUNKS,)), dma((CHUNKS,)),
             dma, dma, dma((CHUNKS, 4, 4)),
@@ -441,7 +495,7 @@
             collective_id=0, has_side_effects=True, vmem_limit_bytes=60 << 20
         ),
         name="ladder",
-    )(amplitudes, integrals, table, bra_pairs, ket_pairs, slot_pair.reshape(16, 128))
+    )(amplitudes, integrals, orbital_irrep, bra_pairs, ket_pairs, slot_pair.reshape(16, 128))
     return result.reshape(BLOCK, N)
 
 

time: 93.1 us -> 87.5 us (0.940)
  Pallas kernels: 90.1 us -> 85.9 us
  local copies, waits for them, and re-layouts: 2.77 us -> 1.47 us
    pallas_call x1, Pallas kernels: 90.1 us -> 85.9 us  [on_device(): pl.pallas_call(kernel, out_shape=jax.ShapeDtypeStruct((BLOCK, 4, 128), F3...]
    reshape x1 -> x0, local copies, waits for them, and re-layouts: 1.3 us -> none  [on_device(): jnp.pad(orbital_irrep, (0, 16 * 128 - orbital_irrep.shape[0]))]
where the time goes in v4:
time: 87.5 us; the launch traced here: 87.3 us
  Pallas kernels  85.9 us (98%)
  local copies, waits for them, and re-layouts  1.47 us (2%)
    pallas_call x1, Pallas kernels, on_device(): pl.pallas_call(kernel, out_shape=jax.ShapeDtypeStruct((BLOCK, 4, 128), F3...  85.9 us

profile of v4, /device:TPU:8, one launch (start us, length us, event | category | flops | bytes accessed | tf_op | source)
XLA Modules:
  0.0 87.3 jit_solution(11648978972907323958)
XLA Ops:
  0.0 85.9 %ladder.1 = f32[32,4,128]{2,1,0:T(4,128)} custom-call(f32[4,32768]{1,0:T(4,128)} %amp_hbm.1, f32[512,512]{1,0:T(8,128)} %ints.1, s32[1600]{0:T(1024)} %table.1, s32[2,512]{1,0:T(2,128)} %bra.1, s32[2,512]{1,0:T(2,128)} %ket.1, s32[16,128]{1,0:T(8,128)} %bitcast.6), custom_call_target="tpu_custom_call" | custom-call | tf_op jit(solution)/shard_map/ladder/pallas_call | solution.py:447
  85.9 1.5 %copy.9 = f32[4,8,4,128]{3,1,2,0:T(8,128)} copy(f32[4,8,4,128]{3,2,1,0:T(4,128)} %bitcast.5) | data formatting | bytes 131072

commit v5 on v4

--- a/solution.py
+++ b/solution.py
@@ -330,11 +330,13 @@
     def step_gather(t):
         @pl.when(holds_rows(t, 0))
         def _():
-            for half in range(2):
+            for turn, half in enumerate((1 - parity, parity)):
                 def put(i, row):
                     core_out[t, half, i] = row
                 gather(t, half, 1 - c, 0, BLOCK, put)
-            remote(core_out.at[t], core_in.at[t], s_c, r_c.at[t], partner_core).start()
+                remote(
+                    core_out.at[t, half], core_in.at[t, half], s_c, r_c.at[t, turn], partner_core
+                ).start()
 
     def piece(i):
         return pl.ds(i * PIECE, PIECE)
@@ -342,7 +344,7 @@
     def step_core(t):
         @pl.when(holds_rows(t, 0))
         def _():
-            wait_bytes(core_in.at[t], r_c.at[t])
+            wait_bytes(core_in.at[t, 1 - parity], r_c.at[t, 0])
 
         @pl.when(holds_rows(t, 1 - parity))
         def _():
@@ -354,6 +356,8 @@
 
         @pl.when(holds_rows(t, 0))
         def _():
+            wait_bytes(core_in.at[t, parity], r_c.at[t, 1])
+
             def put_keep(i, row):
                 y_keep[t, i] = row + core_in[t, parity, i]
             gather(t, parity, c, 0, NARROW, put_keep)
@@ -485,7 +489,7 @@
             dma, dma, dma((CHUNKS, 4, 4)),
             dma, dma((CHUNKS, 2, 4)), dma((CHUNKS, 2)),
             dma, dma((CHUNKS, 4)), dma((CHUNKS,)),
-            dma, dma((16,)),
+            dma, dma((16, 2)),
             dma, dma((16, PIECES)),
             dma, dma((2, 8, PIECES)),
             dma, dma((2, 8)),

time: 87.5 us -> 87.7 us (level)
  no operation moved by 1% of the time
where the time goes in v5:
time: 87.7 us; the launch traced here: 87.5 us
  Pallas kernels  86 us (98%)
  local copies, waits for them, and re-layouts  1.47 us (2%)
    pallas_call x1, Pallas kernels, on_device(): pl.pallas_call(kernel, out_shape=jax.ShapeDtypeStruct((BLOCK, 4, 128), F3...  86 us

profile of v5, /device:TPU:8, one launch (start us, length us, event | category | flops | bytes accessed | tf_op | source)
XLA Modules:
  0.0 87.5 jit_solution(5365350582075447623)
XLA Ops:
  0.0 86.0 %ladder.1 = f32[32,4,128]{2,1,0:T(4,128)} custom-call(f32[4,32768]{1,0:T(4,128)} %amp_hbm.1, f32[512,512]{1,0:T(8,128)} %ints.1, s32[1600]{0:T(1024)} %table.1, s32[2,512]{1,0:T(2,128)} %bra.1, s32[2,512]{1,0:T(2,128)} %ket.1, s32[16,128]{1,0:T(8,128)} %bitcast.6), custom_call_target="tpu_custom_call" | custom-call | tf_op jit(solution)/shard_map/ladder/pallas_call | solution.py:451
  86.0 1.5 %copy.9 = f32[4,8,4,128]{3,1,2,0:T(8,128)} copy(f32[4,8,4,128]{3,2,1,0:T(4,128)} %bitcast.5) | data formatting | bytes 131072
